TPU v7x, 512 devices: a whole 4x8x8 slice. The times are simulated.
512 devices in a mesh: ta: 32 (over x_hi, z, core), gx: 16 (over x_lo, y).
Axes of the slice: x: 4 (x_hi: 2, x_lo: 2; x = x_hi * 2 + x_lo), y: 8, z: 8, core: 2. Of those that a mesh axis runs over, the one named last changes fastest.
Arguments:
- source: float32 [24, 128, 64, 128], P(None, 'ta', 'gx'), may hold values from -6 to 6
- gauge_links: float32 [4, 18, 128, 64, 128], P(None, None, 'ta', 'gx'), may hold values from -1 to 1, as said below
Outputs:
- solution: float32 [24, 128, 64, 128], P(None, 'ta', 'gx')
- residual: float32 [24, 128, 64, 128], P(None, 'ta', 'gx')
Inputs may be any that keep to these rules, and one draw needn't show every extreme that they name: `gauge_links`: every link, read as a 3x3 complex matrix, is special unitary.
All inputs are finite; a program needn't handle non-finite values.
Results may differ from a plain program's by a relative error of at most 0.00014.
Values sent between devices are 32-bit elements; how exact they have to be, the bound alone decides.
A program may use at most 64 MiB of HBM per device.

v0:
```python
import jax
import jax.numpy as jnp
from jax import lax
from jax.experimental import pallas as pl
from jax.experimental.pallas import tpu as pltpu
from jax.sharding import PartitionSpec as P

MR_STEPS = 2
PERM = ((2, 3, 0, 1), (3, 2, 1, 0), (3, 2, 1, 0), (2, 3, 0, 1))
PHASE = (
    (1, 1, 1, 1),
    (1j, 1j, -1j, -1j),
    (-1, 1, 1, -1),
    (1j, -1j, -1j, 1j),
)
MASS_SHIFT = 4.1
DENOM_EPSILON = 1e-6
T, X, Y, Z = range(4)
MESH = pl.DeviceIdType.MESH


def lroll(v, shift):
    return pltpu.roll(v, shift % 128, 1)


def sroll(v, shift):
    shift %= 8
    return v if shift == 0 else pltpu.roll(v, shift, 0)


def plus_phase(x, phase, y):
    if phase == 1:
        return x[0] + y[0], x[1] + y[1]
    if phase == -1:
        return x[0] - y[0], x[1] - y[1]
    if phase == 1j:
        return x[0] - y[1], x[1] + y[0]
    return x[0] + y[1], x[1] - y[0]


def project(v, mu, parity):
    half = []
    for spin in (0, 1):
        phase, partner = parity * PHASE[mu][spin], PERM[mu][spin]
        for colour in range(3):
            at, other = 6 * spin + 2 * colour, 6 * partner + 2 * colour
            half += plus_phase((v[at], v[at + 1]), phase, (v[other], v[other + 1]))
    return half


def reconstruct(acc, half, mu, parity):
    acc = list(acc)
    for spin in range(4):
        phase, source = (1, spin) if spin < 2 else (parity * PHASE[mu][spin], PERM[mu][spin])
        for colour in range(3):
            at, other = 6 * spin + 2 * colour, 6 * source + 2 * colour
            acc[at], acc[at + 1] = plus_phase(
                (acc[at], acc[at + 1]), phase, (half[other], half[other + 1])
            )
    return acc


def times_link(link, half, adjoint):
    out = []
    entry = {}
    for spin in (0, 1):
        for row in range(3):
            re = im = None
            for col in range(3):
                key = 6 * col + 2 * row if adjoint else 6 * row + 2 * col
                if key not in entry:
                    entry[key] = link(key), link(key + 1)
                u_re, u_im = entry[key]
                h_re, h_im = half[6 * spin + 2 * col], half[6 * spin + 2 * col + 1]
                if adjoint:
                    re_term, im_term = u_re * h_re + u_im * h_im, u_re * h_im - u_im * h_re
                else:
                    re_term, im_term = u_re * h_re - u_im * h_im, u_re * h_im + u_im * h_re
                re = re_term if re is None else re + re_term
                im = im_term if im is None else im + im_term
            out += [re, im]
    return out


def kernel(
    counts, src_hbm, links_hbm, sol_hbm, res_hbm,
    src, links, raw, inner, rest, upd, app, sol, res, sent, got,
    in_sem, out_sem, send_sem, recv_sem,
):
    ta, gx = lax.axis_index("ta"), lax.axis_index("gx")
    n_ta, n_gx = counts
    sides = (
        {"ta": lax.rem(ta + n_ta - 1, n_ta)}, {"ta": lax.rem(ta + 1, n_ta)},
        {"gx": lax.rem(gx + n_gx - 1, n_gx)}, {"gx": lax.rem(gx + 1, n_gx)},
    )

    loads = [pltpu.make_async_copy(src_hbm, src, in_sem.at[4])]
    for mu in range(4):
        part = pl.ds(18 * mu, 18)
        loads.append(pltpu.make_async_copy(links_hbm.at[part], links.at[part], in_sem.at[mu]))
    for load in loads:
        load.start()
    barrier = pltpu.get_barrier_semaphore()
    for side in sides:
        pl.semaphore_signal(barrier, inc=1, device_id=side, device_id_type=MESH)

    row = lax.broadcasted_iota(jnp.int32, (8, 128), 0)
    lane = lax.broadcasted_iota(jnp.int32, (8, 128), 1)
    parity = lax.rem(ta + gx, 2)
    x, y, z = row % 4, (lane // 16) % 4, lane % 16
    t = 2 * (lane // 64) + row // 4
    first = (lane // 64 + z // 4 + parity) % 2 == 0
    low_lane, low_row = lane < 64, row < 4
    coords = (t, x, y, z % 4)
    inside = [jnp.where(coords[mu] == 3, 0.0, -0.5) for mu in range(4)]
    face_up = [jnp.where(coords[mu] == 3, 0.5, 0.0) for mu in range(4)]
    face_down = [jnp.where(coords[mu] == 0, 0.5, 0.0) for mu in range(4)]

    def pack(ref, k, colour):
        a, b = ref[k, 0:8, :], ref[k, 8:16, :]
        here = jnp.where(low_lane, a, b)
        there = lroll(jnp.where(low_lane, b, a), 64)
        return jnp.where(first, here, there) if colour == 0 else jnp.where(first, there, here)

    def unpack(ref, k, p0, p1):
        here = jnp.where(first, p0, p1)
        there = lroll(jnp.where(first, p1, p0), 64)
        ref[k, 0:8, :] = jnp.where(low_lane, here, there)
        ref[k, 8:16, :] = jnp.where(low_lane, there, here)

    def pack_links(mu, colour):
        for k in range(18 * mu, 18 * mu + 18):
            value = pack(links, k, colour)
            raw[colour, k] = value
            inner[colour, k] = value * inside[mu]

    def forward(v, mu):
        if mu == Z:
            return lroll(v, -1)
        if mu == Y:
            return lroll(v, -16)
        if mu == X:
            return sroll(v, -1)
        shifted = sroll(v, 4)
        return jnp.where(low_row, shifted, lroll(shifted, 64))

    def backward(v, mu):
        if mu == Z:
            return lroll(v, 1)
        if mu == Y:
            return lroll(v, 16)
        if mu == X:
            return sroll(v, 1)
        shifted = sroll(v, 4)
        return jnp.where(low_row, lroll(shifted, 64), shifted)

    def load(ref, colour):
        return [ref[colour, k] for k in range(24)]

    def block_apply(v, colour):
        acc = [MASS_SHIFT * value for value in v]
        for mu in range(4):
            link = lambda e, mu=mu: inner[colour, 18 * mu + e]
            half = [forward(h, mu) for h in project(v, mu, -1)]
            acc = reconstruct(acc, times_link(link, half, False), mu, -1)
            half = times_link(link, project(v, mu, 1), True)
            acc = reconstruct(acc, [backward(h, mu) for h in half], mu, 1)
        return acc

    def block_sum(v):
        for shift in (4, 2, 1):
            v = v + sroll(v, shift)
        for shift in (64, 32, 16):
            v = v + lroll(v, shift)
        v = v + jnp.where(lane % 2 == 0, lroll(v, -1), lroll(v, 1))
        return v + jnp.where(lane % 4 < 2, lroll(v, -2), lroll(v, 2))

    def minimal_residual(colour):
        for step in range(MR_STEPS):
            v = load(rest, colour)
            a = block_apply(v, colour)
            re = im = norm = None
            for k in range(0, 24, 2):
                a_re, a_im, v_re, v_im = a[k], a[k + 1], v[k], v[k + 1]
                terms = (
                    a_re * v_re + a_im * v_im, a_re * v_im - a_im * v_re, a_re * a_re + a_im * a_im
                )
                if k == 0:
                    re, im, norm = terms
                else:
                    re, im, norm = re + terms[0], im + terms[1], norm + terms[2]
                app[k], app[k + 1] = a_re, a_im
            re, im, norm = block_sum(re), block_sum(im), block_sum(norm)
            norm = norm + DENOM_EPSILON
            re, im = re / norm, im / norm
            for k in range(0, 24, 2):
                v_re, v_im = rest[colour, k], rest[colour, k + 1]
                a_re, a_im = app[k], app[k + 1]
                u_re, u_im = re * v_re - im * v_im, re * v_im + im * v_re
                if step > 0:
                    u_re, u_im = upd[colour, k] + u_re, upd[colour, k + 1] + u_im
                upd[colour, k], upd[colour, k + 1] = u_re, u_im
                rest[colour, k] = v_re - (re * a_re - im * a_im)
                rest[colour, k + 1] = v_im - (re * a_im + im * a_re)

    def squeeze_x(half, at):
        out = []
        for m in range(3):
            v = half[4 * m + at]
            for j in range(4):
                if j != at:
                    v = jnp.where(x == j, sroll(half[4 * m + j], j - at), v)
            out.append(v)
        return out

    def spread_x(three, to):
        return [sroll(three[k // 4], to - k % 4) for k in range(12)]

    def squeeze_t(half, high):
        rows = (row >= 4) if high else low_row
        lanes = (lane >= 64) if high else low_lane
        out = []
        for m in range(3):
            a, b, c, d = half[4 * m : 4 * m + 4]
            one = jnp.where(lanes, a, lroll(b, 64))
            two = jnp.where(lanes, c, lroll(d, 64))
            out.append(jnp.where(rows, one, sroll(two, 4)))
        return out

    def spread_t(three):
        out = []
        for v in three:
            s = sroll(v, 4)
            out += [lroll(s, 64), s, lroll(v, 64), v]
        return out

    def send_faces(colour, turn):
        u = load(upd, colour)
        copies = []
        for slot, (mu, up) in enumerate(((T, False), (T, True), (X, False), (X, True))):
            half = project(u, mu, 1 if up else -1)
            if up:
                half = times_link(lambda e, mu=mu: raw[colour, 18 * mu + e], half, True)
            three = squeeze_t(half, up) if mu == T else squeeze_x(half, 3 if up else 0)
            for m in range(3):
                sent[turn, slot, 8 * m : 8 * m + 8, :] = three[m]
            copy = pltpu.make_async_remote_copy(
                src_ref=sent.at[turn, slot],
                dst_ref=got.at[turn, slot],
                send_sem=send_sem.at[turn, slot],
                recv_sem=recv_sem.at[turn, slot],
                device_id=sides[slot],
                device_id_type=MESH,
            )
            copy.start()
            copies.append(copy)
        return copies

    def local_faces(colour, acc):
        u, other = load(upd, colour), 1 - colour
        for mu in (Y, Z):
            half = project(u, mu, -1)
            if mu == Y:
                half = [lroll(h, 48) for h in half]
            else:
                half = [jnp.where(z == 15, lroll(h, 15), lroll(h, -1)) for h in half]
            half = times_link(lambda e, mu=mu: raw[other, 18 * mu + e], half, False)
            acc = reconstruct(acc, [h * face_up[mu] for h in half], mu, -1)
            half = times_link(lambda e, mu=mu: raw[colour, 18 * mu + e], project(u, mu, 1), True)
            if mu == Y:
                half = [lroll(h, -48) for h in half]
            else:
                half = [jnp.where(z == 0, lroll(h, -15), lroll(h, 1)) for h in half]
            acc = reconstruct(acc, [h * face_down[mu] for h in half], mu, 1)
        return acc

    def far_faces(colour, turn, copies, acc):
        other = 1 - colour
        for slot, (mu, up) in enumerate(((T, False), (T, True), (X, False), (X, True))):
            copies[slot].wait()
            three = [got[turn, slot, 8 * m : 8 * m + 8, :] for m in range(3)]
            if up:
                half = spread_t(three) if mu == T else spread_x(three, 0)
                acc = reconstruct(acc, [h * face_down[mu] for h in half], mu, 1)
            else:
                half = spread_t(three) if mu == T else spread_x(three, 3)
                half = times_link(lambda e, mu=mu: raw[other, 18 * mu + e], half, False)
                acc = reconstruct(acc, [h * face_up[mu] for h in half], mu, -1)
        return acc

    loads[0].wait()
    for k in range(24):
        rest[0, k] = pack(src, k, 0)
    for mu in range(4):
        loads[1 + mu].wait()
        pack_links(mu, 0)
    minimal_residual(0)
    pl.semaphore_wait(barrier, 4)

    copies = send_faces(0, 0)
    for mu in range(4):
        pack_links(mu, 1)
    acc = local_faces(0, [pack(src, k, 1) for k in range(24)])
    acc = far_faces(0, 0, copies, acc)
    for k in range(24):
        rest[1, k] = acc[k]
    minimal_residual(1)

    copies = send_faces(1, 1)
    for k in range(24):
        unpack(sol, k, upd[0, k], upd[1, k])
    store_sol = pltpu.make_async_copy(sol, sol_hbm, out_sem.at[0])
    store_sol.start()
    acc = local_faces(1, load(rest, 0))
    acc = far_faces(1, 1, copies, acc)
    for k in range(24):
        unpack(res, k, acc[k], rest[1, k])
    store_res = pltpu.make_async_copy(res, res_hbm, out_sem.at[1])
    store_res.start()
    store_sol.wait()
    store_res.wait()


def solution(mesh):
    counts = mesh.shape["ta"], mesh.shape["gx"]

    def local(source, gauge_links):
        spinor = jax.ShapeDtypeStruct((24, 16, 128), jnp.float32)
        vmem = lambda *shape: pltpu.VMEM(shape, jnp.float32)
        out = pl.pallas_call(
            lambda *refs: kernel(counts, *refs),
            out_shape=(spinor, spinor),
            in_specs=[pl.BlockSpec(memory_space=pl.ANY)] * 2,
            out_specs=(pl.BlockSpec(memory_space=pl.ANY),) * 2,
            scratch_shapes=[
                vmem(24, 16, 128),
                vmem(72, 16, 128),
                vmem(2, 72, 8, 128),
                vmem(2, 72, 8, 128),
                vmem(2, 24, 8, 128),
                vmem(2, 24, 8, 128),
                vmem(24, 8, 128),
                vmem(24, 16, 128),
                vmem(24, 16, 128),
                vmem(2, 4, 24, 128),
                vmem(2, 4, 24, 128),
                pltpu.SemaphoreType.DMA((5,)),
                pltpu.SemaphoreType.DMA((2,)),
                pltpu.SemaphoreType.DMA((2, 4)),
                pltpu.SemaphoreType.DMA((2, 4)),
            ],
            compiler_params=pltpu.CompilerParams(
                collective_id=0, has_side_effects=True, vmem_limit_bytes=24 << 20
            ),
            name="schwarz",
        )(source.reshape(24, 16, 128), gauge_links.reshape(72, 16, 128))
        return tuple(value.reshape(24, 4, 4, 128) for value in out)

    return jax.shard_map(
        local,
        mesh=mesh,
        in_specs=(P(None, "ta", "gx", None), P(None, None, "ta", "gx", None)),
        out_specs=(P(None, "ta", "gx", None), P(None, "ta", "gx", None)),
        check_vma=False,
    )
```

profile of v0, /device:TPU:56, one launch (start us, length us, event | category | flops | bytes accessed | tf_op | source)
XLA Modules:
  0.0 27.1 jit_solution(7246265460791430854)
XLA Ops:
  0.6 0.0 copy-start
  0.6 1.1 %copy-done = f32[4,18,4,4,128]{4,3,2,1,0:T(4,128)S(1)} copy-done((f32[4,18,4,4,128]{4,3,2,1,0:T(4,128)S(1)}, f32[4,18,4,4,128]{4,3,2,1,0:T(4,128)}, u32[]{:S(2)}) %copy-start) | copy-done | bytes 589848
  1.7 0.0 copy-start.1
  1.7 0.9 %copy-done.1 = f32[24,4,4,128]{3,2,1,0:T(4,128)S(1)} copy-done((f32[24,4,4,128]{3,2,1,0:T(4,128)S(1)}, f32[24,4,4,128]{3,2,1,0:T(4,128)}, u32[]{:S(2)}) %copy-start.1) | copy-done | bytes 196632
  2.6 23.1 %schwarz.1 = (f32[24,16,128]{2,1,0:T(8,128)S(1)}, f32[24,16,128]{2,1,0:T(8,128)S(1)}) custom-call(f32[24,16,128]{2,1,0:T(8,128)S(1)} %bitcast.7, f32[72,16,128]{2,1,0:T(8,128)S(1)} %bitcast.4), custom_call_target="tpu_custom_call" | custom-call | tf_op jit(solution)/shard_map/schwarz/pallas_call | solution.py:330
  25.7 0.7 %copy.6 = f32[24,4,4,128]{3,2,1,0:T(4,128)} copy(f32[24,4,4,128]{3,2,1,0:T(4,128)S(1)} %bitcast.6) | data formatting | bytes 393216
  26.4 0.7 %copy.7 = f32[24,4,4,128]{3,2,1,0:T(4,128)} copy(f32[24,4,4,128]{3,2,1,0:T(4,128)S(1)} %bitcast.5) | data formatting | bytes 393216
Async XLA Ops:
  0.6 1.1 %copy-start = (f32[4,18,4,4,128]{4,3,2,1,0:T(4,128)S(1)}, f32[4,18,4,4,128]{4,3,2,1,0:T(4,128)}, u32[]{:S(2)}) copy-start(f32[4,18,4,4,128]{4,3,2,1,0:T(4,128)} %param.3) | copy-start | bytes 1769476
  1.7 0.9 %copy-start.1 = (f32[24,4,4,128]{3,2,1,0:T(4,128)S(1)}, f32[24,4,4,128]{3,2,1,0:T(4,128)}, u32[]{:S(2)}) copy-start(f32[24,4,4,128]{3,2,1,0:T(4,128)} %param.2) | copy-start | bytes 589828
where the time goes:
time: 27.3 us; the launch traced here: 27.1 us
  Pallas kernels  23.1 us (85%)
  local copies, waits for them, and re-layouts  3.34 us (12%)
  between operations  0.65 us (2%)
    pallas_call x1, Pallas kernels, local(): pl.pallas_call(lambda *refs: kernel(counts, *refs), out_shape=(spinor, sp...  23.1 us
    unnamed x6, local copies, waits for them, and re-layouts  3.34 us

commit v1 on v0

--- a/solution.py
+++ b/solution.py
@@ -82,10 +82,32 @@
     return out
 
 
+def first_colour(lane):
+    parity = lax.rem(lax.axis_index("ta") + lax.axis_index("gx"), 2)
+    return (lane // 64 + lane % 16 // 4 + parity) % 2 == 0
+
+
+def store_kernel(upd, rest, sol_hbm, res_hbm, sol, res, out_sem):
+    lane = lax.broadcasted_iota(jnp.int32, (8, 128), 1)
+    first, low_lane = first_colour(lane), lane < 64
+    stores = []
+    for n, (packed, plain, out) in enumerate(((upd, sol, sol_hbm), (rest, res, res_hbm))):
+        for k in range(24):
+            p0, p1 = packed[0, k], packed[1, k]
+            here = jnp.where(first, p0, p1)
+            there = lroll(jnp.where(first, p1, p0), 64)
+            plain[k, 0:8, :] = jnp.where(low_lane, here, there)
+            plain[k, 8:16, :] = jnp.where(low_lane, there, here)
+        store = pltpu.make_async_copy(plain, out, out_sem.at[n])
+        store.start()
+        stores.append(store)
+    for store in stores:
+        store.wait()
+
+
 def kernel(
-    counts, src_hbm, links_hbm, sol_hbm, res_hbm,
-    src, links, raw, inner, rest, upd, app, sol, res, sent, got,
-    in_sem, out_sem, send_sem, recv_sem,
+    counts, src_hbm, links_hbm, upd, rest,
+    src, links, raw, inner, app, sent, got, in_sem, send_sem, recv_sem,
 ):
     ta, gx = lax.axis_index("ta"), lax.axis_index("gx")
     n_ta, n_gx = counts
@@ -106,10 +128,9 @@
 
     row = lax.broadcasted_iota(jnp.int32, (8, 128), 0)
     lane = lax.broadcasted_iota(jnp.int32, (8, 128), 1)
-    parity = lax.rem(ta + gx, 2)
     x, y, z = row % 4, (lane // 16) % 4, lane % 16
     t = 2 * (lane // 64) + row // 4
-    first = (lane // 64 + z // 4 + parity) % 2 == 0
+    first = first_colour(lane)
     low_lane, low_row = lane < 64, row < 4
     coords = (t, x, y, z % 4)
     inside = [jnp.where(coords[mu] == 3, 0.0, -0.5) for mu in range(4)]
@@ -121,12 +142,6 @@
         here = jnp.where(low_lane, a, b)
         there = lroll(jnp.where(low_lane, b, a), 64)
         return jnp.where(first, here, there) if colour == 0 else jnp.where(first, there, here)
-
-    def unpack(ref, k, p0, p1):
-        here = jnp.where(first, p0, p1)
-        there = lroll(jnp.where(first, p1, p0), 64)
-        ref[k, 0:8, :] = jnp.where(low_lane, here, there)
-        ref[k, 8:16, :] = jnp.where(low_lane, there, here)
 
     def pack_links(mu, colour):
         for k in range(18 * mu, 18 * mu + 18):
@@ -307,45 +322,34 @@
     minimal_residual(1)
 
     copies = send_faces(1, 1)
-    for k in range(24):
-        unpack(sol, k, upd[0, k], upd[1, k])
-    store_sol = pltpu.make_async_copy(sol, sol_hbm, out_sem.at[0])
-    store_sol.start()
     acc = local_faces(1, load(rest, 0))
     acc = far_faces(1, 1, copies, acc)
     for k in range(24):
-        unpack(res, k, acc[k], rest[1, k])
-    store_res = pltpu.make_async_copy(res, res_hbm, out_sem.at[1])
-    store_res.start()
-    store_sol.wait()
-    store_res.wait()
+        rest[0, k] = acc[k]
 
 
 def solution(mesh):
     counts = mesh.shape["ta"], mesh.shape["gx"]
 
     def local(source, gauge_links):
-        spinor = jax.ShapeDtypeStruct((24, 16, 128), jnp.float32)
+        spinor = pltpu.HBM((24, 16, 128), jnp.float32)
         vmem = lambda *shape: pltpu.VMEM(shape, jnp.float32)
-        out = pl.pallas_call(
+        packed = pltpu.VMEM((2, 24, 8, 128), jnp.float32)
+        hbm, in_vmem = pl.BlockSpec(memory_space=pltpu.HBM), pl.BlockSpec(memory_space=pltpu.VMEM)
+        upd, rest = pl.pallas_call(
             lambda *refs: kernel(counts, *refs),
-            out_shape=(spinor, spinor),
-            in_specs=[pl.BlockSpec(memory_space=pl.ANY)] * 2,
-            out_specs=(pl.BlockSpec(memory_space=pl.ANY),) * 2,
+            out_shape=(packed, packed),
+            in_specs=[hbm, hbm],
+            out_specs=(in_vmem, in_vmem),
             scratch_shapes=[
                 vmem(24, 16, 128),
                 vmem(72, 16, 128),
                 vmem(2, 72, 8, 128),
                 vmem(2, 72, 8, 128),
-                vmem(2, 24, 8, 128),
-                vmem(2, 24, 8, 128),
                 vmem(24, 8, 128),
-                vmem(24, 16, 128),
-                vmem(24, 16, 128),
                 vmem(2, 4, 24, 128),
                 vmem(2, 4, 24, 128),
                 pltpu.SemaphoreType.DMA((5,)),
-                pltpu.SemaphoreType.DMA((2,)),
                 pltpu.SemaphoreType.DMA((2, 4)),
                 pltpu.SemaphoreType.DMA((2, 4)),
             ],
@@ -353,7 +357,24 @@
                 collective_id=0, has_side_effects=True, vmem_limit_bytes=24 << 20
             ),
             name="schwarz",
-        )(source.reshape(24, 16, 128), gauge_links.reshape(72, 16, 128))
+        )(
+            pltpu.with_memory_space_constraint(source.reshape(24, 16, 128), pltpu.HBM),
+            pltpu.with_memory_space_constraint(gauge_links.reshape(72, 16, 128), pltpu.HBM),
+        )
+        out = pl.pallas_call(
+            store_kernel,
+            out_shape=(spinor, spinor),
+            in_specs=[in_vmem, in_vmem],
+            out_specs=(hbm, hbm),
+            scratch_shapes=[
+                vmem(24, 16, 128), vmem(24, 16, 128), pltpu.SemaphoreType.DMA((2,)),
+            ],
+            compiler_params=pltpu.CompilerParams(vmem_limit_bytes=4 << 20),
+            name="store",
+        )(
+            pltpu.with_memory_space_constraint(upd, pltpu.VMEM),
+            pltpu.with_memory_space_constraint(rest, pltpu.VMEM),
+        )
         return tuple(value.reshape(24, 4, 4, 128) for value in out)
 
     return jax.shard_map(

time: 27.3 us -> 24 us (0.88)
  the two profiles are of different devices: /device:TPU:56 before, /device:TPU:2 now
where the time goes in v1:
time: 24 us; the launch traced here: 23.9 us
  Pallas kernels  23.2 us (97%)
  between operations  0.64 us (3%)
    pallas_call x1, Pallas kernels, local(): pl.pallas_call(lambda *refs: kernel(counts, *refs), out_shape=(packed, pa...  22.4 us
    pallas_call x1, Pallas kernels, local(): pl.pallas_call(store_kernel, out_shape=(spinor, spinor), in_specs=[in_vme...  0.87 us

profile of v1, /device:TPU:2, one launch (start us, length us, event | category | flops | bytes accessed | tf_op | source)
XLA Modules:
  0.0 23.9 jit_solution(8844600773644692276)
XLA Ops:
  0.6 22.4 %schwarz.1 = (f32[2,24,8,128]{3,2,1,0:T(8,128)S(1)}, f32[2,24,8,128]{3,2,1,0:T(8,128)S(1)}) custom-call(f32[24,16,128]{2,1,0:T(8,128)} %bitcast.5, f32[72,16,128]{2,1,0:T(8,128)} %bitcast.4), custom_call_target="tpu_custom_call" | custom-call | tf_op jit(solution)/shard_map/schwarz/pallas_call | solution.py:339
  23.0 0.9 %store.1 = (f32[24,16,128]{2,1,0:T(8,128)}, f32[24,16,128]{2,1,0:T(8,128)}) custom-call(f32[2,24,8,128]{3,2,1,0:T(8,128)S(1)} %get-tuple-element.6.upd, f32[2,24,8,128]{3,2,1,0:T(8,128)S(1)} %get-tuple-element.7.rest), custom_call_target="tpu_custom_call" | custom-call | tf_op jit(solution)/shard_map/store/pallas_call | solution.py:364

commit v2 on v0

v2 whole, which is shorter than its diff:
```python
import jax
import jax.numpy as jnp
from jax import lax
from jax.experimental import pallas as pl
from jax.experimental.pallas import tpu as pltpu
from jax.sharding import PartitionSpec as P

MR_STEPS = 2
PERM = ((2, 3, 0, 1), (3, 2, 1, 0), (3, 2, 1, 0), (2, 3, 0, 1))
PHASE = (
    (1, 1, 1, 1),
    (1j, 1j, -1j, -1j),
    (-1, 1, 1, -1),
    (1j, -1j, -1j, 1j),
)
MASS_SHIFT = 4.1
DENOM_EPSILON = 1e-6
T, X, Y, Z = range(4)
MESH = pl.DeviceIdType.MESH


def lroll(v, shift):
    return pltpu.roll(v, shift % 128, 1)


def sroll(v, shift):
    shift %= 8
    return v if shift == 0 else pltpu.roll(v, shift, 0)


def plus_phase(x, phase, y):
    if phase == 1:
        return x[0] + y[0], x[1] + y[1]
    if phase == -1:
        return x[0] - y[0], x[1] - y[1]
    if phase == 1j:
        return x[0] - y[1], x[1] + y[0]
    return x[0] + y[1], x[1] - y[0]


def project(v, mu, parity):
    half = []
    for spin in (0, 1):
        phase, partner = parity * PHASE[mu][spin], PERM[mu][spin]
        for colour in range(3):
            at, other = 6 * spin + 2 * colour, 6 * partner + 2 * colour
            half += plus_phase((v[at], v[at + 1]), phase, (v[other], v[other + 1]))
    return half


def reconstruct(acc, half, mu, parity):
    acc = list(acc)
    for spin in range(4):
        phase, source = (1, spin) if spin < 2 else (parity * PHASE[mu][spin], PERM[mu][spin])
        for colour in range(3):
            at, other = 6 * spin + 2 * colour, 6 * source + 2 * colour
            acc[at], acc[at + 1] = plus_phase(
                (acc[at], acc[at + 1]), phase, (half[other], half[other + 1])
            )
    return acc


def times_link(link, half, adjoint):
    out = []
    entry = {}
    for spin in (0, 1):
        for row in range(3):
            re = im = None
            for col in range(3):
                key = 6 * col + 2 * row if adjoint else 6 * row + 2 * col
                if key not in entry:
                    entry[key] = link(key), link(key + 1)
                u_re, u_im = entry[key]
                h_re, h_im = half[6 * spin + 2 * col], half[6 * spin + 2 * col + 1]
                if adjoint:
                    re_term, im_term = u_re * h_re + u_im * h_im, u_re * h_im - u_im * h_re
                else:
                    re_term, im_term = u_re * h_re - u_im * h_im, u_re * h_im + u_im * h_re
                re = re_term if re is None else re + re_term
                im = im_term if im is None else im + im_term
            out += [re, im]
    return out


def store_kernel(sol, res, sol_hbm, res_hbm, out_sem):
    stores = (
        pltpu.make_async_copy(sol, sol_hbm, out_sem.at[0]),
        pltpu.make_async_copy(res, res_hbm, out_sem.at[1]),
    )
    for store in stores:
        store.start()
    for store in stores:
        store.wait()


def times_link_by_three(link, half, adjoint):
    entry = {}
    sums = [half[n] + half[n + 1] for n in range(0, 12, 2)]
    out = []
    for spin in (0, 1):
        for row in range(3):
            one = two = three = None
            for col in range(3):
                key = (col, row) if adjoint else (row, col)
                if key not in entry:
                    entry[key] = link(3 * key[0] + key[1])
                u_re, u_plus, u_minus = entry[key]
                h_re, h_im = half[6 * spin + 2 * col], half[6 * spin + 2 * col + 1]
                if adjoint:
                    terms = u_re * sums[3 * spin + col], u_plus * h_re, u_minus * h_im
                else:
                    terms = u_re * sums[3 * spin + col], u_minus * h_re, u_plus * h_im
                if col == 0:
                    one, two, three = terms
                else:
                    one, two, three = one + terms[0], two + terms[1], three + terms[2]
            out += [one + three, one - two] if adjoint else [one - three, one + two]
    return out


def kernel(
    counts, src_hbm, links_hbm, sol, res,
    src, links, raw, inner, upd, rest, app, sent, got, in_sem, send_sem, recv_sem,
):
    ta, gx = lax.axis_index("ta"), lax.axis_index("gx")
    n_ta, n_gx = counts
    sides = (
        {"ta": lax.rem(ta + n_ta - 1, n_ta)}, {"ta": lax.rem(ta + 1, n_ta)},
        {"gx": lax.rem(gx + n_gx - 1, n_gx)}, {"gx": lax.rem(gx + 1, n_gx)},
    )

    barrier = pltpu.get_barrier_semaphore()
    for side in sides:
        pl.semaphore_signal(barrier, inc=1, device_id=side, device_id_type=MESH)
    loads = [pltpu.make_async_copy(src_hbm, src, in_sem.at[4])]
    for mu in range(4):
        part = pl.ds(18 * mu, 18)
        loads.append(pltpu.make_async_copy(links_hbm.at[part], links.at[part], in_sem.at[mu]))
    for load in loads:
        load.start()

    row = lax.broadcasted_iota(jnp.int32, (8, 128), 0)
    lane = lax.broadcasted_iota(jnp.int32, (8, 128), 1)
    x, y, z = row % 4, (lane // 16) % 4, lane % 16
    t = 2 * (lane // 64) + row // 4
    first = (lane // 64 + z // 4 + lax.rem(ta + gx, 2)) % 2 == 0
    low_lane, low_row = lane < 64, row < 4
    coords = (t, x, y, z % 4)
    lane_row = lax.broadcasted_iota(jnp.int32, (128, 128), 0)
    lane_col = lax.broadcasted_iota(jnp.int32, (128, 128), 1)
    same_block = (lane_row % 16 // 4 == lane_col % 16 // 4).astype(jnp.bfloat16)
    inside = [jnp.where(coords[mu] == 3, 0.0, -0.5 / MASS_SHIFT) for mu in range(4)]
    face_up = [jnp.where(coords[mu] == 3, 0.5, 0.0) for mu in range(4)]
    face_down = [jnp.where(coords[mu] == 0, 0.5, 0.0) for mu in range(4)]

    def pack(ref, k, colour):
        a, b = ref[k, 0:8, :], ref[k, 8:16, :]
        here = jnp.where(low_lane, a, b)
        there = lroll(jnp.where(low_lane, b, a), 64)
        return jnp.where(first, here, there) if colour == 0 else jnp.where(first, there, here)

    def unpack(ref, k, p0, p1):
        here = jnp.where(first, p0, p1)
        there = lroll(jnp.where(first, p1, p0), 64)
        ref[k, 0:8, :] = jnp.where(low_lane, here, there)
        ref[k, 8:16, :] = jnp.where(low_lane, there, here)

    def pack_links(mu, colour):
        for k in range(9 * mu, 9 * mu + 9):
            re, im = pack(links, 2 * k, colour), pack(links, 2 * k + 1, colour)
            raw[colour, 2 * k], raw[colour, 2 * k + 1] = re, im
            re, im = re * inside[mu], im * inside[mu]
            inner[colour, 3 * k] = re
            inner[colour, 3 * k + 1] = im + re
            inner[colour, 3 * k + 2] = im - re

    def forward(v, mu):
        if mu == Z:
            return lroll(v, -1)
        if mu == Y:
            return lroll(v, -16)
        if mu == X:
            return sroll(v, -1)
        shifted = sroll(v, 4)
        return jnp.where(low_row, shifted, lroll(shifted, 64))

    def backward(v, mu):
        if mu == Z:
            return lroll(v, 1)
        if mu == Y:
            return lroll(v, 16)
        if mu == X:
            return sroll(v, 1)
        shifted = sroll(v, 4)
        return jnp.where(low_row, lroll(shifted, 64), shifted)

    def load(ref, colour):
        return [ref[colour, k] for k in range(24)]

    def store(ref, colour, values):
        for k in range(24):
            ref[colour, k] = values[k]

    def block_apply(v, colour):
        acc = v
        for mu in range(4):
            link = lambda e, mu=mu: [inner[colour, 27 * mu + 3 * e + n] for n in range(3)]
            half = [forward(h, mu) for h in project(v, mu, -1)]
            acc = reconstruct(acc, times_link_by_three(link, half, False), mu, -1)
            half = times_link_by_three(link, project(v, mu, 1), True)
            acc = reconstruct(acc, [backward(h, mu) for h in half], mu, 1)
        return acc

    def block_sums(stats):
        for shift in (4, 2, 1):
            stats = [v + sroll(v, shift) for v in stats]
        rows = jnp.where(row == 0, stats[0], jnp.where(row == 1, stats[1], stats[2]))
        pieces = []
        for _ in range(3):
            pieces.append(rows.astype(jnp.bfloat16).astype(jnp.float32))
            rows = rows - pieces[-1]
        pieces.append(jnp.zeros_like(rows))
        split = jnp.concatenate(pieces).astype(jnp.bfloat16)
        sums = jnp.dot(split, same_block, preferred_element_type=jnp.float32)
        sums = sums[0:8] + sums[8:16] + sums[16:24]
        return [jnp.broadcast_to(sums[n : n + 1], (8, 128)) for n in range(3)]

    def coefficient(a, v):
        re = im = norm = None
        for k in range(0, 24, 2):
            a_re, a_im, v_re, v_im = a[k], a[k + 1], v[k], v[k + 1]
            terms = a_re * v_re + a_im * v_im, a_re * v_im - a_im * v_re, a_re * a_re + a_im * a_im
            if k == 0:
                re, im, norm = terms
            else:
                re, im, norm = re + terms[0], im + terms[1], norm + terms[2]
        re, im, norm = block_sums([re, im, norm])
        norm = norm + DENOM_EPSILON / MASS_SHIFT**2
        alpha = re / norm, im / norm
        return alpha, [value * (1 / MASS_SHIFT) for value in alpha]

    def plus_times(x, sign, alpha, y):
        out = []
        for k in range(0, 24, 2):
            re = alpha[0] * y[k] - alpha[1] * y[k + 1]
            im = alpha[0] * y[k + 1] + alpha[1] * y[k]
            if x is None:
                out += [re, im]
            elif sign > 0:
                out += [x[k] + re, x[k + 1] + im]
            else:
                out += [x[k] - re, x[k + 1] - im]
        return out

    def minimal_residual(colour):
        v = load(rest, colour)
        a = block_apply(v, colour)
        store(app, 0, a)
        b = block_apply(a, colour)
        alpha, scaled = coefficient(a, v)
        v, a = load(rest, colour), load(app, 0)
        update = plus_times(None, 1, scaled, v)
        v = plus_times(v, -1, alpha, a)
        a = plus_times(a, -1, alpha, b)
        store(app, 0, a)
        store(rest, colour, v)
        alpha, scaled = coefficient(a, v)
        update = plus_times(update, 1, scaled, load(rest, colour))
        store(upd, colour, update)
        return update, alpha

    def squeeze_x(half, at):
        out = []
        for m in range(3):
            v = half[4 * m + at]
            for j in range(4):
                if j != at:
                    v = jnp.where(x == j, sroll(half[4 * m + j], j - at), v)
            out.append(v)
        return out

    def spread_x(three, to):
        return [sroll(three[k // 4], to - k % 4) for k in range(12)]

    def squeeze_t(half, high):
        rows = (row >= 4) if high else low_row
        lanes = (lane >= 64) if high else low_lane
        out = []
        for m in range(3):
            a, b, c, d = half[4 * m : 4 * m + 4]
            one = jnp.where(lanes, a, lroll(b, 64))
            two = jnp.where(lanes, c, lroll(d, 64))
            out.append(jnp.where(rows, one, sroll(two, 4)))
        return out

    def spread_t(three):
        out = []
        for v in three:
            s = sroll(v, 4)
            out += [lroll(s, 64), s, lroll(v, 64), v]
        return out

    def faces(u, colour, slot):
        mu, up = slot // 2, slot % 2 == 1
        half = project(u, mu, 1 if up else -1)
        if up:
            half = times_link(lambda e: raw[colour, 18 * mu + e], half, True)
        three = squeeze_t(half, up) if mu == T else squeeze_x(half, 3 if up else 0)
        for m in range(3):
            sent[colour, slot, 8 * m : 8 * m + 8, :] = three[m]

    def send(colour, slots):
        @pl.when(ta >= 0)
        def _():
            for slot in slots:
                pltpu.make_async_remote_copy(
                    src_ref=sent.at[colour, slot],
                    dst_ref=got.at[colour, slot],
                    send_sem=send_sem.at[0],
                    recv_sem=recv_sem.at[colour, min(slot, 2)],
                    device_id=sides[slot],
                    device_id_type=MESH,
                ).start()

    def await_face(colour, slot, count=1):
        part = got.at[colour, pl.ds(slot, count)]
        pltpu.make_async_copy(part, part, recv_sem.at[colour, slot]).wait()

    def local_faces(u, colour, acc):
        other = 1 - colour
        for mu in (Y, Z):
            half = project(u, mu, -1)
            if mu == Y:
                half = [lroll(h, 48) for h in half]
            else:
                half = [jnp.where(z == 15, lroll(h, 15), lroll(h, -1)) for h in half]
            half = times_link(lambda e, mu=mu: raw[other, 18 * mu + e], half, False)
            acc = reconstruct(acc, [h * face_up[mu] for h in half], mu, -1)
            half = times_link(lambda e, mu=mu: raw[colour, 18 * mu + e], project(u, mu, 1), True)
            if mu == Y:
                half = [lroll(h, -48) for h in half]
            else:
                half = [jnp.where(z == 0, lroll(h, -15), lroll(h, 1)) for h in half]
            acc = reconstruct(acc, [h * face_down[mu] for h in half], mu, 1)
        return acc

    def add_face(acc, colour, slot):
        mu, up = slot // 2, slot % 2 == 1
        three = [got[colour, slot, 8 * m : 8 * m + 8, :] for m in range(3)]
        if up:
            half = spread_t(three) if mu == T else spread_x(three, 0)
            return reconstruct(acc, [h * face_down[mu] for h in half], mu, 1)
        half = spread_t(three) if mu == T else spread_x(three, 3)
        half = times_link(lambda e: raw[1 - colour, 18 * mu + e], half, False)
        return reconstruct(acc, [h * face_up[mu] for h in half], mu, -1)

    loads[0].wait()
    for k in range(24):
        rest[0, k] = pack(src, k, 0)
    for mu in range(4):
        loads[1 + mu].wait()
    for mu in range(4):
        pack_links(mu, 0)

    update, alpha = minimal_residual(0)
    for slot in range(4):
        faces(update, 0, slot)
    pl.semaphore_wait(barrier, 4)
    send(0, (0, 1, 2, 3))
    for k in range(24):
        rest[1, k] = pack(src, k, 1)
    for mu in range(4):
        pack_links(mu, 1)
    store(rest, 0, plus_times(load(rest, 0), -1, alpha, load(app, 0)))
    acc = local_faces(load(upd, 0), 0, load(rest, 1))
    store(rest, 1, acc)
    await_face(0, 2, 2)
    acc = add_face(add_face(load(rest, 1), 0, 2), 0, 3)
    store(rest, 1, acc)
    await_face(0, 1)
    await_face(0, 0)
    store(rest, 1, add_face(add_face(load(rest, 1), 0, 1), 0, 0))

    update, alpha = minimal_residual(1)
    faces(update, 1, 1)
    send(1, (1,))
    faces(update, 1, 3)
    send(1, (3,))
    for slot in (2, 0):
        faces(update, 1, slot)
    send(1, (2, 0))
    store(rest, 1, plus_times(load(rest, 1), -1, alpha, load(app, 0)))
    for k in range(24):
        unpack(sol, k, upd[0, k], upd[1, k])
    store(rest, 0, local_faces(load(upd, 1), 1, load(rest, 0)))
    await_face(1, 2, 2)
    store(rest, 0, add_face(add_face(load(rest, 0), 1, 2), 1, 3))
    await_face(1, 0)
    acc = add_face(load(rest, 0), 1, 0)
    for k in range(24):
        unpack(res, k, acc[k], rest[1, k])
    pltpu.make_async_copy(sent, sent, send_sem.at[0]).wait()
    at_zero = jnp.where(first & low_row, 0.5, 0.0)
    await_face(1, 1)
    half = []
    for m in range(3):
        v = got[1, 1, 8 * m : 8 * m + 8, :]
        s = sroll(v, 4)
        v_far, s_far = lroll(v, 64), lroll(s, 64)
        half += [
            jnp.where(low_lane, s_far, s), jnp.where(low_lane, s, s_far),
            jnp.where(low_lane, v_far, v), jnp.where(low_lane, v, v_far),
        ]
    acc = [res[k, 0:8, :] for k in range(24)]
    acc = reconstruct(acc, [h * at_zero for h in half], T, 1)
    for k in range(24):
        res[k, 0:8, :] = acc[k]


def solution(mesh):
    counts = mesh.shape["ta"], mesh.shape["gx"]

    def local(source, gauge_links):
        spinor = pltpu.HBM((24, 16, 128), jnp.float32)
        vmem = lambda *shape: pltpu.VMEM(shape, jnp.float32)
        plain = pltpu.VMEM((24, 16, 128), jnp.float32)
        hbm, in_vmem = pl.BlockSpec(memory_space=pltpu.HBM), pl.BlockSpec(memory_space=pltpu.VMEM)
        out = pl.pallas_call(
            lambda *refs: kernel(counts, *refs),
            out_shape=(plain, plain),
            in_specs=[hbm, hbm],
            out_specs=(in_vmem, in_vmem),
            scratch_shapes=[
                vmem(24, 16, 128),
                vmem(72, 16, 128),
                vmem(2, 72, 8, 128),
                vmem(2, 108, 8, 128),
                vmem(2, 24, 8, 128),
                vmem(2, 24, 8, 128),
                vmem(1, 24, 8, 128),
                vmem(2, 4, 24, 128),
                vmem(2, 4, 24, 128),
                pltpu.SemaphoreType.DMA((5,)),
                pltpu.SemaphoreType.DMA((1,)),
                pltpu.SemaphoreType.DMA((2, 3)),
            ],
            compiler_params=pltpu.CompilerParams(
                collective_id=0, has_side_effects=True, vmem_limit_bytes=24 << 20
            ),
            name="schwarz",
        )(
            pltpu.with_memory_space_constraint(source.reshape(24, 16, 128), pltpu.HBM),
            pltpu.with_memory_space_constraint(gauge_links.reshape(72, 16, 128), pltpu.HBM),
        )
        out = pl.pallas_call(
            store_kernel,
            out_shape=(spinor, spinor),
            in_specs=[in_vmem, in_vmem],
            out_specs=(hbm, hbm),
            scratch_shapes=[pltpu.SemaphoreType.DMA((2,))],
            compiler_params=pltpu.CompilerParams(vmem_limit_bytes=4 << 20),
            name="store",
        )(*(pltpu.with_memory_space_constraint(value, pltpu.VMEM) for value in out))
        return tuple(value.reshape(24, 4, 4, 128) for value in out)

    return jax.shard_map(
        local,
        mesh=mesh,
        in_specs=(P(None, "ta", "gx", None), P(None, None, "ta", "gx", None)),
        out_specs=(P(None, "ta", "gx", None), P(None, "ta", "gx", None)),
        check_vma=False,
    )
```

time: 27.3 us -> 23 us (0.84)
  the two profiles are of different devices: /device:TPU:56 before, /device:TPU:2 now
where the time goes in v2:
time: 23 us; the launch traced here: 22.8 us
  Pallas kernels  22.2 us (97%)
  between operations  0.64 us (3%)
    pallas_call x1, Pallas kernels, local(): pl.pallas_call(lambda *refs: kernel(counts, *refs), out_shape=(plain, pla...  21.4 us
    pallas_call x1, Pallas kernels, local(): pl.pallas_call(store_kernel, out_shape=(spinor, spinor), in_specs=[in_vme...  0.76 us

profile of v2, /device:TPU:2, one launch (start us, length us, event | category | flops | bytes accessed | tf_op | source)
XLA Modules:
  0.0 22.8 jit_solution(17783446120603607174)
XLA Ops:
  0.6 21.4 %schwarz.1 = (f32[24,16,128]{2,1,0:T(8,128)S(1)}, f32[24,16,128]{2,1,0:T(8,128)S(1)}) custom-call(f32[24,16,128]{2,1,0:T(8,128)} %bitcast.5, f32[72,16,128]{2,1,0:T(8,128)} %bitcast.4), custom_call_target="tpu_custom_call" | custom-call | tf_op jit(solution)/shard_map/schwarz/pallas_call | solution.py:428
  22.1 0.8 %store.1 = (f32[24,16,128]{2,1,0:T(8,128)}, f32[24,16,128]{2,1,0:T(8,128)}) custom-call(f32[24,16,128]{2,1,0:T(8,128)S(1)} %get-tuple-element.6.sol, f32[24,16,128]{2,1,0:T(8,128)S(1)} %get-tuple-element.7.res), custom_call_target="tpu_custom_call" | custom-call | tf_op jit(solution)/shard_map/store/pallas_call | solution.py:455

commit v3 on v2

--- a/solution.py
+++ b/solution.py
@@ -145,6 +145,7 @@
     t = 2 * (lane // 64) + row // 4
     first = (lane // 64 + z // 4 + lax.rem(ta + gx, 2)) % 2 == 0
     low_lane, low_row = lane < 64, row < 4
+    own = (first & low_lane, first & ~low_lane), (~first & low_lane, ~first & ~low_lane)
     coords = (t, x, y, z % 4)
     lane_row = lax.broadcasted_iota(jnp.int32, (128, 128), 0)
     lane_col = lax.broadcasted_iota(jnp.int32, (128, 128), 1)
@@ -155,9 +156,9 @@
 
     def pack(ref, k, colour):
         a, b = ref[k, 0:8, :], ref[k, 8:16, :]
-        here = jnp.where(low_lane, a, b)
         there = lroll(jnp.where(low_lane, b, a), 64)
-        return jnp.where(first, here, there) if colour == 0 else jnp.where(first, there, here)
+        own_a, own_b = own[colour]
+        return jnp.where(own_a, a, jnp.where(own_b, b, there))
 
     def unpack(ref, k, p0, p1):
         here = jnp.where(first, p0, p1)
@@ -216,13 +217,12 @@
             stats = [v + sroll(v, shift) for v in stats]
         rows = jnp.where(row == 0, stats[0], jnp.where(row == 1, stats[1], stats[2]))
         pieces = []
-        for _ in range(3):
+        for _ in range(2):
             pieces.append(rows.astype(jnp.bfloat16).astype(jnp.float32))
             rows = rows - pieces[-1]
-        pieces.append(jnp.zeros_like(rows))
         split = jnp.concatenate(pieces).astype(jnp.bfloat16)
         sums = jnp.dot(split, same_block, preferred_element_type=jnp.float32)
-        sums = sums[0:8] + sums[8:16] + sums[16:24]
+        sums = sums[0:8] + sums[8:16]
         return [jnp.broadcast_to(sums[n : n + 1], (8, 128)) for n in range(3)]
 
     def coefficient(a, v):
@@ -264,10 +264,31 @@
         a = plus_times(a, -1, alpha, b)
         store(app, 0, a)
         store(rest, colour, v)
+        store(upd, colour, update)
+        parts = {}
+        for up in (False, True):
+            halves = [t_half(w, colour, up) for w in (update, v)]
+            turned = []
+            for n in range(0, 12, 2):
+                turned += [-halves[1][n + 1], halves[1][n]]
+            parts[up] = [squeeze_t(half, up) for half in (*halves, turned)]
         alpha, scaled = coefficient(a, v)
-        update = plus_times(update, 1, scaled, load(rest, colour))
+        for up in (True, False):
+            for m in range(3):
+                so_far, along, across = (part[m] for part in parts[up])
+                sent[colour, int(up), 8 * m : 8 * m + 8, :] = (
+                    so_far + scaled[0] * along + scaled[1] * across
+                )
+        return alpha, scaled
+
+    def finish(colour, scaled):
+        update = plus_times(load(upd, colour), 1, scaled, load(rest, colour))
         store(upd, colour, update)
-        return update, alpha
+        return update
+
+    def t_half(v, colour, up):
+        half = project(v, T, 1 if up else -1)
+        return times_link(lambda e: raw[colour, e], half, True) if up else half
 
     def squeeze_x(half, at):
         out = []
@@ -300,12 +321,12 @@
             out += [lroll(s, 64), s, lroll(v, 64), v]
         return out
 
-    def faces(u, colour, slot):
-        mu, up = slot // 2, slot % 2 == 1
-        half = project(u, mu, 1 if up else -1)
+    def x_face(u, colour, slot):
+        up = slot == 3
+        half = project(u, X, 1 if up else -1)
         if up:
-            half = times_link(lambda e: raw[colour, 18 * mu + e], half, True)
-        three = squeeze_t(half, up) if mu == T else squeeze_x(half, 3 if up else 0)
+            half = times_link(lambda e: raw[colour, 18 + e], half, True)
+        three = squeeze_x(half, 3 if up else 0)
         for m in range(3):
             sent[colour, slot, 8 * m : 8 * m + 8, :] = three[m]
 
@@ -362,11 +383,13 @@
     for mu in range(4):
         pack_links(mu, 0)
 
-    update, alpha = minimal_residual(0)
-    for slot in range(4):
-        faces(update, 0, slot)
+    alpha, scaled = minimal_residual(0)
     pl.semaphore_wait(barrier, 4)
-    send(0, (0, 1, 2, 3))
+    send(0, (1, 0))
+    update = finish(0, scaled)
+    for slot in (3, 2):
+        x_face(update, 0, slot)
+    send(0, (3, 2))
     for k in range(24):
         rest[1, k] = pack(src, k, 1)
     for mu in range(4):
@@ -381,14 +404,12 @@
     await_face(0, 0)
     store(rest, 1, add_face(add_face(load(rest, 1), 0, 1), 0, 0))
 
-    update, alpha = minimal_residual(1)
-    faces(update, 1, 1)
-    send(1, (1,))
-    faces(update, 1, 3)
-    send(1, (3,))
-    for slot in (2, 0):
-        faces(update, 1, slot)
-    send(1, (2, 0))
+    alpha, scaled = minimal_residual(1)
+    send(1, (1, 0))
+    update = finish(1, scaled)
+    for slot in (3, 2):
+        x_face(update, 1, slot)
+        send(1, (slot,))
     store(rest, 1, plus_times(load(rest, 1), -1, alpha, load(app, 0)))
     for k in range(24):
         unpack(sol, k, upd[0, k], upd[1, k])

time: 23 us -> 22.8 us (level)
  no operation moved by 1% of the time
where the time goes in v3:
time: 22.8 us; the launch traced here: 22.6 us
  Pallas kernels  22 us (96%)
  between operations  0.64 us (3%)
    pallas_call x1, Pallas kernels, local(): pl.pallas_call(lambda *refs: kernel(counts, *refs), out_shape=(plain, pla...  21.2 us
    pallas_call x1, Pallas kernels, local(): pl.pallas_call(store_kernel, out_shape=(spinor, spinor), in_specs=[in_vme...  0.76 us

profile of v3, /device:TPU:2, one launch (start us, length us, event | category | flops | bytes accessed | tf_op | source)
XLA Modules:
  0.0 22.6 jit_solution(3785431716592668521)
XLA Ops:
  0.6 21.2 %schwarz.1 = (f32[24,16,128]{2,1,0:T(8,128)S(1)}, f32[24,16,128]{2,1,0:T(8,128)S(1)}) custom-call(f32[24,16,128]{2,1,0:T(8,128)} %bitcast.5, f32[72,16,128]{2,1,0:T(8,128)} %bitcast.4), custom_call_target="tpu_custom_call" | custom-call | tf_op jit(solution)/shard_map/schwarz/pallas_call | solution.py:449
  21.9 0.8 %store.1 = (f32[24,16,128]{2,1,0:T(8,128)}, f32[24,16,128]{2,1,0:T(8,128)}) custom-call(f32[24,16,128]{2,1,0:T(8,128)S(1)} %get-tuple-element.6.sol, f32[24,16,128]{2,1,0:T(8,128)S(1)} %get-tuple-element.7.res), custom_call_target="tpu_custom_call" | custom-call | tf_op jit(solution)/shard_map/store/pallas_call | solution.py:476

commit v4 on v3

--- a/solution.py
+++ b/solution.py
@@ -145,7 +145,9 @@
     t = 2 * (lane // 64) + row // 4
     first = (lane // 64 + z // 4 + lax.rem(ta + gx, 2)) % 2 == 0
     low_lane, low_row = lane < 64, row < 4
-    own = (first & low_lane, first & ~low_lane), (~first & low_lane, ~first & ~low_lane)
+    lanes_of = (
+        (first & low_lane, first & ~low_lane), (~first & low_lane, ~first & ~low_lane)
+    )
     coords = (t, x, y, z % 4)
     lane_row = lax.broadcasted_iota(jnp.int32, (128, 128), 0)
     lane_col = lax.broadcasted_iota(jnp.int32, (128, 128), 1)
@@ -157,7 +159,7 @@
     def pack(ref, k, colour):
         a, b = ref[k, 0:8, :], ref[k, 8:16, :]
         there = lroll(jnp.where(low_lane, b, a), 64)
-        own_a, own_b = own[colour]
+        own_a, own_b = lanes_of[colour]
         return jnp.where(own_a, a, jnp.where(own_b, b, there))
 
     def unpack(ref, k, p0, p1):
@@ -338,13 +340,13 @@
                     src_ref=sent.at[colour, slot],
                     dst_ref=got.at[colour, slot],
                     send_sem=send_sem.at[0],
-                    recv_sem=recv_sem.at[colour, min(slot, 2)],
+                    recv_sem=recv_sem.at[colour, slot],
                     device_id=sides[slot],
                     device_id_type=MESH,
                 ).start()
 
-    def await_face(colour, slot, count=1):
-        part = got.at[colour, pl.ds(slot, count)]
+    def await_face(colour, slot):
+        part = got.at[colour, slot]
         pltpu.make_async_copy(part, part, recv_sem.at[colour, slot]).wait()
 
     def local_faces(u, colour, acc):
@@ -397,7 +399,8 @@
     store(rest, 0, plus_times(load(rest, 0), -1, alpha, load(app, 0)))
     acc = local_faces(load(upd, 0), 0, load(rest, 1))
     store(rest, 1, acc)
-    await_face(0, 2, 2)
+    await_face(0, 2)
+    await_face(0, 3)
     acc = add_face(add_face(load(rest, 1), 0, 2), 0, 3)
     store(rest, 1, acc)
     await_face(0, 1)
@@ -414,10 +417,10 @@
     for k in range(24):
         unpack(sol, k, upd[0, k], upd[1, k])
     store(rest, 0, local_faces(load(upd, 1), 1, load(rest, 0)))
-    await_face(1, 2, 2)
-    store(rest, 0, add_face(add_face(load(rest, 0), 1, 2), 1, 3))
     await_face(1, 0)
-    acc = add_face(load(rest, 0), 1, 0)
+    store(rest, 0, add_face(load(rest, 0), 1, 0))
+    await_face(1, 2)
+    acc = add_face(load(rest, 0), 1, 2)
     for k in range(24):
         unpack(res, k, acc[k], rest[1, k])
     pltpu.make_async_copy(sent, sent, send_sem.at[0]).wait()
@@ -436,6 +439,15 @@
     acc = reconstruct(acc, [h * at_zero for h in half], T, 1)
     for k in range(24):
         res[k, 0:8, :] = acc[k]
+    at_zero = jnp.where(first & (x == 0), 0.5, 0.0)
+    await_face(1, 3)
+    near = spread_x([got[1, 3, 8 * m : 8 * m + 8, :] for m in range(3)], 0)
+    far = [lroll(h, 64) for h in near]
+    for rows, own, other in ((slice(0, 8), near, far), (slice(8, 16), far, near)):
+        half = [jnp.where(low_lane, p, q) * at_zero for p, q in zip(own, other)]
+        acc = reconstruct([res[k, rows, :] for k in range(24)], half, X, 1)
+        for k in range(24):
+            res[k, rows, :] = acc[k]
 
 
 def solution(mesh):
@@ -463,7 +475,7 @@
                 vmem(2, 4, 24, 128),
                 pltpu.SemaphoreType.DMA((5,)),
                 pltpu.SemaphoreType.DMA((1,)),
-                pltpu.SemaphoreType.DMA((2, 3)),
+                pltpu.SemaphoreType.DMA((2, 4)),
             ],
             compiler_params=pltpu.CompilerParams(
                 collective_id=0, has_side_effects=True, vmem_limit_bytes=24 << 20

time: 22.8 us -> 22.6 us (level)
  no operation moved by 1% of the time
where the time goes in v4:
time: 22.6 us; the launch traced here: 22.4 us
  Pallas kernels  21.8 us (96%)
  between operations  0.64 us (3%)
    pallas_call x1, Pallas kernels, local(): pl.pallas_call(lambda *refs: kernel(counts, *refs), out_shape=(plain, pla...  21 us
    pallas_call x1, Pallas kernels, local(): pl.pallas_call(store_kernel, out_shape=(spinor, spinor), in_specs=[in_vme...  0.76 us

profile of v4, /device:TPU:2, one launch (start us, length us, event | category | flops | bytes accessed | tf_op | source)
XLA Modules:
  0.0 22.4 jit_solution(3725148344170020395)
XLA Ops:
  0.6 21.0 %schwarz.1 = (f32[24,16,128]{2,1,0:T(8,128)S(1)}, f32[24,16,128]{2,1,0:T(8,128)S(1)}) custom-call(f32[24,16,128]{2,1,0:T(8,128)} %bitcast.5, f32[72,16,128]{2,1,0:T(8,128)} %bitcast.4), custom_call_target="tpu_custom_call" | custom-call | tf_op jit(solution)/shard_map/schwarz/pallas_call | solution.py:461
  21.7 0.8 %store.1 = (f32[24,16,128]{2,1,0:T(8,128)}, f32[24,16,128]{2,1,0:T(8,128)}) custom-call(f32[24,16,128]{2,1,0:T(8,128)S(1)} %get-tuple-element.6.sol, f32[24,16,128]{2,1,0:T(8,128)S(1)} %get-tuple-element.7.res), custom_call_target="tpu_custom_call" | custom-call | tf_op jit(solution)/shard_map/store/pallas_call | solution.py:488

commit v5 on v4

--- a/solution.py
+++ b/solution.py
@@ -215,17 +215,15 @@
         return acc
 
     def block_sums(stats):
+        rows = jnp.concatenate(stats)
+        high = rows.astype(jnp.bfloat16)
+        low = (rows - high.astype(jnp.float32)).astype(jnp.bfloat16)
+        split = jnp.concatenate([high.astype(jnp.float32), low.astype(jnp.float32)]).astype(jnp.bfloat16)
+        sums = jnp.dot(split, same_block, preferred_element_type=jnp.float32)
+        stats = [sums[8 * n : 8 * n + 8] + sums[24 + 8 * n : 32 + 8 * n] for n in range(3)]
         for shift in (4, 2, 1):
             stats = [v + sroll(v, shift) for v in stats]
-        rows = jnp.where(row == 0, stats[0], jnp.where(row == 1, stats[1], stats[2]))
-        pieces = []
-        for _ in range(2):
-            pieces.append(rows.astype(jnp.bfloat16).astype(jnp.float32))
-            rows = rows - pieces[-1]
-        split = jnp.concatenate(pieces).astype(jnp.bfloat16)
-        sums = jnp.dot(split, same_block, preferred_element_type=jnp.float32)
-        sums = sums[0:8] + sums[8:16]
-        return [jnp.broadcast_to(sums[n : n + 1], (8, 128)) for n in range(3)]
+        return stats
 
     def coefficient(a, v):
         re = im = norm = None

time: 22.6 us -> 22.6 us (level)
  no operation moved by 1% of the time
where the time goes in v5:
time: 22.6 us; the launch traced here: 22.4 us
  Pallas kernels  21.8 us (96%)
  between operations  0.64 us (3%)
    pallas_call x1, Pallas kernels, local(): pl.pallas_call(lambda *refs: kernel(counts, *refs), out_shape=(plain, pla...  21 us
    pallas_call x1, Pallas kernels, local(): pl.pallas_call(store_kernel, out_shape=(spinor, spinor), in_specs=[in_vme...  0.76 us

profile of v5, /device:TPU:2, one launch (start us, length us, event | category | flops | bytes accessed | tf_op | source)
XLA Modules:
  0.0 22.4 jit_solution(5048713856845242419)
XLA Ops:
  0.6 21.0 %schwarz.1 = (f32[24,16,128]{2,1,0:T(8,128)S(1)}, f32[24,16,128]{2,1,0:T(8,128)S(1)}) custom-call(f32[24,16,128]{2,1,0:T(8,128)} %bitcast.5, f32[72,16,128]{2,1,0:T(8,128)} %bitcast.4), custom_call_target="tpu_custom_call" | custom-call | tf_op jit(solution)/shard_map/schwarz/pallas_call | solution.py:459
  21.7 0.8 %store.1 = (f32[24,16,128]{2,1,0:T(8,128)}, f32[24,16,128]{2,1,0:T(8,128)}) custom-call(f32[24,16,128]{2,1,0:T(8,128)S(1)} %get-tuple-element.6.sol, f32[24,16,128]{2,1,0:T(8,128)S(1)} %get-tuple-element.7.res), custom_call_target="tpu_custom_call" | custom-call | tf_op jit(solution)/shard_map/store/pallas_call | solution.py:486
